TPU v7x, 32 devices: a whole 2x2x4 slice. The times are simulated.
32 devices in a mesh: shard: 8 (over z, y), replica: 4 (over x, core).
Axes of the slice: x: 2, y: 2, z: 4, core: 2. Of those that a mesh axis runs over, the one named last changes fastest.
Arguments:
- grads: bfloat16 [16384, 512], P('shard'), may hold values from -1.5 to 1.5
- piece_position: int32 [32], replicated, may hold values from 0 to 31, each once
- owner: int32 [32], replicated, may hold values from 0 to 31, as said below
- stat_left: float32 [8, 4, 1, 512, 512], P('shard', 'replica'), may hold values from -1 to 8, as said below
- stat_right: float32 [8, 4, 1, 512, 512], P('shard', 'replica'), may hold values from -1 to 8, as said below
- root_left: bfloat16 [8, 4, 1, 512, 512], P('shard', 'replica'), may hold values from -1 to 4, as said below
- root_right: bfloat16 [8, 4, 1, 512, 512], P('shard', 'replica'), may hold values from -1 to 4, as said below
Outputs:
- new_left: float32 [8, 4, 1, 512, 512], P('shard', 'replica')
- new_right: float32 [8, 4, 1, 512, 512], P('shard', 'replica')
- directions: bfloat16 [16384, 512], P('shard')
Inputs may be any that keep to these rules, and one draw needn't show every extreme that they name: `owner`: entries are distinct; entry v names slot v % 1 of the device with shard index (v) // the replica axis's size and replica index (v) % that size. Some device owns 1 block. `stat_left`: Symmetric; diagonal entries positive. `stat_right`: Symmetric; diagonal entries positive. `root_left`: Symmetric; diagonal entries positive. `root_right`: Symmetric; diagonal entries positive.
All inputs are finite; a program needn't handle non-finite values.
Results may differ from a plain program's by a relative error of at most 0.0049.
Values may be sent and summed in bfloat16 or wider, within the bound.
A program may use at most 64 MiB of HBM per device.

v0:
```python
import jax
import jax.numpy as jnp
from jax import lax
from jax.sharding import PartitionSpec as P

BETA = 0.95


def slot_update(block_grad, old_left, old_right, slot_left, slot_right):
    gram_left = jnp.einsum(
        "cij,ckj->cik", block_grad, block_grad, preferred_element_type=jnp.float32
    )
    gram_right = jnp.einsum(
        "cji,cjk->cik", block_grad, block_grad, preferred_element_type=jnp.float32
    )
    next_left = BETA * old_left + (1.0 - BETA) * gram_left
    next_right = BETA * old_right + (1.0 - BETA) * gram_right
    half = jnp.einsum(
        "cij,cjk->cik", slot_left, block_grad, preferred_element_type=jnp.float32
    ).astype(jnp.bfloat16)
    direction = jnp.einsum(
        "cij,cjk->cik", half, slot_right, preferred_element_type=jnp.float32
    ).astype(jnp.bfloat16)
    return (next_left, next_right, direction)


def body(grads, piece_position, owner, stat_left, stat_right, root_left, root_right):
    block_count = piece_position.shape[0]
    block_width = grads.shape[1]
    piece_rows = grads.shape[0] // block_count
    shard_count = lax.axis_size("shard")
    group_count = lax.axis_size("replica")
    slot_count = stat_left.shape[2]
    my_shard = lax.axis_index("shard")
    my_group = lax.axis_index("replica")
    pieces = grads.reshape(block_count, piece_rows, block_width)
    shard_ids = jnp.arange(shard_count, dtype=jnp.int32)
    slot_ids = jnp.arange(slot_count, dtype=jnp.int32)
    targets = (shard_ids[None, :] * group_count + my_group) * slot_count + slot_ids[:, None]
    matches = owner[None, None, :] == targets[:, :, None]
    present = jnp.any(matches, axis=2)
    chosen = jnp.argmax(matches.astype(jnp.int32), axis=2)
    outgoing = jnp.where(
        present[:, :, None, None], pieces[piece_position[chosen]], jnp.zeros((), jnp.bfloat16)
    )
    incoming = lax.all_to_all(outgoing, "shard", split_axis=1, concat_axis=1, tiled=True)
    block_grad = incoming.reshape(slot_count, block_width, block_width)
    old_left = stat_left.reshape(slot_count, block_width, block_width)
    old_right = stat_right.reshape(slot_count, block_width, block_width)
    slot_left = root_left.reshape(slot_count, block_width, block_width)
    slot_right = root_right.reshape(slot_count, block_width, block_width)
    my_slots = (my_shard * group_count + my_group) * slot_count + slot_ids
    occupied = jnp.any(owner[None, :] == my_slots[:, None], axis=1)
    next_left, next_right, direction = slot_update(
        block_grad, old_left, old_right, slot_left, slot_right
    )
    new_left = jnp.where(occupied[:, None, None], next_left, old_left)
    new_right = jnp.where(occupied[:, None, None], next_right, old_right)
    returned = lax.all_to_all(
        direction.reshape(slot_count, shard_count, piece_rows, block_width),
        "shard",
        split_axis=1,
        concat_axis=1,
        tiled=True,
    )
    owner_device = owner // slot_count
    owner_slot = owner % slot_count
    owner_shard = owner_device // group_count
    owner_group = owner_device % group_count
    empty_layout = jnp.zeros((block_count, piece_rows, block_width), jnp.bfloat16)
    everyone = lax.all_gather(returned[None], "replica", axis=0, tiled=True)
    flattened = everyone.reshape(group_count * slot_count * shard_count, piece_rows, block_width)
    picked = flattened[(owner_group * slot_count + owner_slot) * shard_count + owner_shard]
    result = empty_layout.at[piece_position].set(picked)
    return (
        new_left.reshape(stat_left.shape),
        new_right.reshape(stat_right.shape),
        result.reshape(block_count * piece_rows, block_width),
    )


def solution(mesh):
    return jax.shard_map(
        body,
        mesh=mesh,
        in_specs=(
            P("shard", None),
            P(),
            P(),
            P("shard", "replica", None, None, None),
            P("shard", "replica", None, None, None),
            P("shard", "replica", None, None, None),
            P("shard", "replica", None, None, None),
        ),
        out_specs=(
            P("shard", "replica", None, None, None),
            P("shard", "replica", None, None, None),
            P("shard", None),
        ),
        check_vma=False,
    )
```

profile of v0, /device:TPU:0, one launch (start us, length us, event | category | flops | bytes accessed | tf_op | source)
XLA Modules:
  0.0 92.9 jit_solution(9857630243714365112)
XLA Ops:
  7.2 0.0 copy-start
  7.2 0.0 all-gather.3.cloned.1.call-start
  7.2 1.0 %compare_reduce_fusion = pred[8]{0:T(512)(128)(4,1)S(1)} fusion(s32[32]{0:T(128)} %param.9, s32[8]{0:T(128)S(1)} %multiply_add_fusion), kind=kLoop, calls=%fused_computation.22 | loop fusion | flops 504 | bytes 168 | tf_op jit(solution)/shard_map/reduce_or | solution.py:41
  8.2 1.4 %fusion.11 = (s32[1,8]{1,0:T(1,128)}, s32[1,8]{1,0:T(1,128)S(1)}) fusion(s32[32]{0:T(128)} %param.9, s32[8]{0:T(128)S(1)} %multiply_add_fusion), kind=kLoop, calls=%fused_computation.23 | loop fusion | flops 2248 | bytes 224 | tf_op jit(solution)/shard_map/body/reduce | solution.py:42
  9.6 1.3 %gather_fusion = s32[8]{0:T(128)S(1)} fusion(s32[32]{0:T(128)} %param.8, s32[1024]{0:T(1024)S(1)} %pad_clamp_fusion.2), kind=kCustom, calls=%fused_computation | custom fusion | bytes 96 | tf_op jit(solution)/shard_map/gather | solution.py:44
  10.9 0.0 copy-done
  10.9 0.6 gather_fusion.1
  11.5 0.1 bitcast_select_fusion
  11.6 21.6 %all_to_all.10 = bf16[1,8,64,512]{3,2,0,1:T(8,128)(2,1)S(1)} all-to-all(bf16[1,8,64,512]{3,2,0,1:T(8,128)(2,1)S(1)} %bitcast_select_fusion), channel_id=1, replica_groups=mesh['shard'=8,'replica'=4] {'shard'}, dimensions={1} | all-to-all | bytes 1048576 | tf_op jit(solution)/shard_map/all_to_all | solution.py:46
  33.2 0.0 copy-start.2
  33.2 2.1 %convolution_convert_fusion = bf16[512,512]{1,0:T(8,128)(2,1)S(1)} fusion(bf16[512,512]{1,0:T(8,128)(2,1)S(1)} %bitcast.56, bf16[1,1,1,512,512]{4,3,2,1,0:T(8,128)(2,1)} %param.13, bf16[1,1,1,512,512]{4,3,2,1,0:T(8,128)(2,1)} %param.12), kind=kOutput, calls=%fused_computation.13 | convolution fusion | flops 537395200 | bytes 2097152 | tf_op jit(solution)/shard_map/cij,cjk->cik/dot_general | solution.py:21
  35.3 17.6 %all_to_all.11 = bf16[1,8,64,512]{3,2,0,1:T(8,128)(2,1)} all-to-all(bf16[1,8,64,512]{3,2,0,1:T(8,128)(2,1)S(1)} %bitcast.60), channel_id=1, replica_groups=mesh['shard'=8,'replica'=4] {'shard'}, dimensions={1} | all-to-all | bytes 1048576 | tf_op jit(solution)/shard_map/all_to_all | solution.py:59
  52.9 0.0 all-gather.3.cloned.1.call-update
  53.0 0.0 copy-done.2
  53.0 0.0 copy-start.3
  53.0 0.6 compare_reduce_fusion.1
  53.7 0.0 copy-done.1
  53.7 3.4 %fusion.6 = f32[1,1,1,512,512]{4,3,2,1,0:T(8,128)} fusion(bf16[512,512]{1,0:T(8,128)(2,1)S(1)} %bitcast.57, f32[1,1,1,512,512]{4,3,2,1,0:T(8,128)} %param.10, pred[]{:T(512)} %compare_reduce_fusion.1), kind=kOutput, calls=%fused_computation.12 | convolution fusion | flops 269484032 | bytes 2621441 | tf_op jit(solution)/shard_map/cij,ckj->cik/dot_general | solution.py:10
  57.0 0.0 copy-done.3
  57.0 2.1 %fusion.3 = f32[1,1,1,512,512]{4,3,2,1,0:T(8,128)} fusion(f32[1,1,1,512,512]{4,3,2,1,0:T(8,128)S(1)} %copy-done.3, bf16[1,8,64,512]{3,2,0,1:T(8,128)(2,1)S(1)} %all_to_all.10, pred[]{:T(512)} %compare_reduce_fusion.1), kind=kOutput, calls=%fused_computation.8 | convolution fusion | flops 269484032 | bytes 2621441 | tf_op jit(solution)/shard_map/cji,cjk->cik/dot_general | solution.py:13
  59.2 15.6 %all-gather.3.cloned.1.call-done = bf16[4,8,64,512]{3,2,1,0:T(8,128)(2,1)} async-done(((bf16[1,8,64,512]{3,2,1,0:T(8,128)(2,1)}), bf16[4,8,64,512]{3,2,1,0:T(8,128)(2,1)}) %all-gather.3.cloned.1.call-update) | async-done | bytes 2097168 | tf_op jit(solution)/shard_map/all_gather | solution.py:71
  74.8 3.6 %gather_fusion.2 = bf16[32,64,512]{2,1,0:T(8,128)(2,1)} fusion(bf16[32,64,512]{2,1,0:T(8,128)(2,1)} %bitcast.58, s32[1024]{0:T(1024)S(1)} %pad_clamp_fusion), kind=kCustom, calls=%fused_computation.2 | custom fusion | bytes 4194432 | tf_op jit(solution)/shard_map/gather | solution.py:73
  78.3 1.6 %broadcast_in_dim.50 = bf16[32,64,512]{2,1,0:T(8,128)(2,1)} broadcast(bf16[]{:T(256)} %constant.69.clone.1), dimensions={} | broadcast | bytes 2097154 | tf_op jit(solution)/shard_map/broadcast_in_dim | solution.py:70
  79.9 6.2 %scatter_fusion = bf16[32,64,512]{2,1,0:T(8,128)(2,1)} fusion(bf16[32,64,512]{2,1,0:T(8,128)(2,1)} %broadcast_in_dim.50, s32[32]{0:T(128)S(1)} %compare_select_fusion.1, bf16[32,64,512]{2,1,0:T(8,128)(2,1)} %gather_fusion.2), kind=kCustom, calls=%fused_computation.3 | custom fusion | bytes 6291584 | tf_op jit(solution)/shard_map/scatter | solution.py:74
  (9 shorter events, 0.1 us)
Async XLA Ops:
  7.2 3.7 %copy-start = (bf16[2048,512]{1,0:T(8,128)(2,1)S(1)}, bf16[2048,512]{1,0:T(8,128)(2,1)}, u32[]{:S(2)}) copy-start(bf16[2048,512]{1,0:T(8,128)(2,1)} %param.7) | copy-start | bytes 6291460
  7.2 67.6 %all-gather.3.cloned.1.call-start = ((), (), s32[]{:S(2)}) async-start(), calls=%async_computation.2 | async-start | bytes 2621440 | tf_op jit(solution)/shard_map/all_gather | solution.py:71
  33.2 19.8 %copy-start.2 = (s32[32]{0:T(128)S(1)}, s32[32]{0:T(128)}, u32[]{:S(2)}) copy-start(s32[32]{0:T(128)} %param.9) | copy-start | bytes 388
  33.2 20.4 %copy-start.1 = (s32[32]{0:T(128)S(1)}, s32[32]{0:T(128)}, u32[]{:S(2)}) copy-start(s32[32]{0:T(128)} %param.8) | copy-start | bytes 388
  53.0 4.1 %copy-start.3 = (f32[1,1,1,512,512]{4,3,2,1,0:T(8,128)S(1)}, f32[1,1,1,512,512]{4,3,2,1,0:T(8,128)}, u32[]{:S(2)}) copy-start(f32[1,1,1,512,512]{4,3,2,1,0:T(8,128)} %param.11) | copy-start | bytes 3145732
Sparse Core Ops, SparseCore 0:
  53.1 21.6 all-gather.2
where the time goes:
time: 93.3 us; the launch traced here: 92.9 us
  blocking collectives  39.3 us (42%)
  waiting for transfers between devices  15.6 us (17%)
  between operations  14.1 us (15%)
  local copies, waits for them, and re-layouts  13.2 us (14%)
  matrix products  7.56 us (8%)
  other arithmetic  3.13 us (3%)
    all_to_all x1, blocking collectives, body(): lax.all_to_all(outgoing, 'shard', split_axis=1, concat_axis=1, tiled=True)  21.6 us
    all_to_all x1, blocking collectives, body(): lax.all_to_all(direction.reshape(slot_count, shard_count, piece_rows, blo...  17.6 us
    all_gather x1, waiting for transfers between devices, body(): everyone = lax.all_gather(returned[None], 'replica', axis=0, tiled=True)  15.6 us
    scatter x1, local copies, waits for them, and re-layouts, body(): result = empty_layout.at[piece_position].set(picked)  6.2 us
    gather x1, local copies, waits for them, and re-layouts, body(): flattened[(owner_group * slot_count + owner_slot) * shard_count + owner_s...  3.56 us
    dot_general x1, matrix products, slot_update(): jnp.einsum('cij,ckj->cik', block_grad, block_grad, preferred_element_type...  3.36 us
    dot_general x1, matrix products, slot_update(): jnp.einsum('cji,cjk->cik', block_grad, block_grad, preferred_element_type...  2.14 us
    dot_general x1, matrix products, slot_update(): jnp.einsum('cij,cjk->cik', half, slot_right, preferred_element_type=jnp.f...  2.07 us
  transfers between devices with their start and end apart: 1, of which 1 were waited for; matrix products, arithmetic and copies ran while one was open for 7% of the time, Pallas kernels for 0%

commit v1 on v0

v1 whole, which is shorter than its diff:
```python
import functools

import jax
import jax.numpy as jnp
from jax import lax
from jax.experimental import pallas as pl
from jax.experimental.pallas import tpu as pltpu
from jax.sharding import PartitionSpec as P

BETA = 0.95
MESH = pl.DeviceIdType.MESH
CORES = 2


def exchange_kernel(
    shards, groups,
    owner, position, grads, root_left, root_right,
    block_out, gathered,
    grads_v, left_v, right_v, outgoing, block, direction,
    load_sem, block_sem, own_sem,
    send1, recv1, send2, recv2, send_sib, recv_sib, send_x, recv_x, send_xs, recv_xs,
):
    me = lax.axis_index("shard")
    group = lax.axis_index("replica")
    chips = groups // CORES
    sibling = group + 1 - 2 * (group % CORES)
    width = grads.shape[2]

    barrier = pltpu.get_barrier_semaphore()
    for k in range(1, shards):
        pl.semaphore_signal(
            barrier, inc=1, device_id={"shard": (me + k) % shards, "replica": group},
            device_id_type=MESH)
    pl.semaphore_signal(
        barrier, inc=1, device_id={"shard": me, "replica": sibling}, device_id_type=MESH)
    for j in range(1, chips):
        pl.semaphore_signal(
            barrier, inc=1,
            device_id={"shard": me, "replica": (group + CORES * j) % groups},
            device_id_type=MESH)

    load_grads = pltpu.make_async_copy(grads, grads_v, load_sem.at[0])
    load_grads.start()
    load_left = pltpu.make_async_copy(root_left, left_v, load_sem.at[1])
    load_left.start()
    load_right = pltpu.make_async_copy(root_right, right_v, load_sem.at[2])
    load_right.start()

    targets = [((me + k) % shards) * groups + group for k in range(shards)]

    def find(b, found):
        o, p = owner[b], position[b]
        return tuple(jnp.where(o == t, p, f) for t, f in zip(targets, found))

    found = lax.fori_loop(0, owner.shape[0], find, (jnp.int32(0),) * shards)

    load_grads.wait()
    for k in range(1, shards):
        outgoing[k] = grads_v[found[k]]
    block[me] = grads_v[found[0]]

    pl.semaphore_wait(barrier, shards - 1 + 1 + chips - 1)

    first = []
    for k in range(1, shards):
        copy = pltpu.make_async_remote_copy(
            src_ref=outgoing.at[k], dst_ref=block.at[me],
            send_sem=send1.at[k], recv_sem=recv1.at[k],
            device_id={"shard": (me + k) % shards, "replica": group}, device_id_type=MESH)
        copy.start()
        first.append(copy)
    load_left.wait()
    load_right.wait()
    for copy in first:
        copy.wait_recv()

    keep = pltpu.make_async_copy(block, block_out, block_sem)
    keep.start()
    whole = block[...].reshape(-1, width)
    half = jnp.dot(left_v[...], whole, preferred_element_type=jnp.float32).astype(jnp.bfloat16)
    direction[...] = jnp.dot(
        half, right_v[...], preferred_element_type=jnp.float32
    ).astype(jnp.bfloat16).reshape(direction.shape)

    pending = []
    second = [None]
    for k in range(1, shards):
        copy = pltpu.make_async_remote_copy(
            src_ref=direction.at[(me + k) % shards], dst_ref=gathered.at[me * groups + group],
            send_sem=send2.at[k], recv_sem=recv2.at[k],
            device_id={"shard": (me + k) % shards, "replica": group}, device_id_type=MESH)
        copy.start()
        second.append(copy)
        pending.append(copy)

    across = [None] * shards
    to_sibling = []

    def forward(k, source, slot):
        across[k] = []
        for j in range(1, chips):
            copy = pltpu.make_async_remote_copy(
                src_ref=source, dst_ref=gathered.at[slot],
                send_sem=send_x.at[k, j], recv_sem=recv_x.at[k, j],
                device_id={"shard": me, "replica": (group + CORES * j) % groups},
                device_id_type=MESH)
            copy.start()
            across[k].append(copy)
            pending.append(copy)
        copy = pltpu.make_async_remote_copy(
            src_ref=source, dst_ref=gathered.at[slot],
            send_sem=send_sib.at[k], recv_sem=recv_sib.at[k],
            device_id={"shard": me, "replica": sibling}, device_id_type=MESH)
        copy.start()
        to_sibling.append(copy)
        pending.append(copy)

    def pass_on(k):
        source_shard = (me + shards - k) % shards
        for j in range(1, chips):
            across[k][j - 1].wait_recv()
            slot = source_shard * groups + (group + groups - CORES * j) % groups
            copy = pltpu.make_async_remote_copy(
                src_ref=gathered.at[slot], dst_ref=gathered.at[slot],
                send_sem=send_xs.at[k, j], recv_sem=recv_xs.at[k, j],
                device_id={"shard": me, "replica": sibling}, device_id_type=MESH)
            copy.start()
            to_sibling.append(copy)
            pending.append(copy)

    forward(0, direction.at[me], me * groups + group)
    own = pltpu.make_async_copy(direction.at[me], gathered.at[me * groups + group], own_sem)
    own.start()
    for k in range(1, shards):
        second[k].wait_recv()
        slot = ((me + shards - k) % shards) * groups + group
        forward(k, gathered.at[slot], slot)
        pass_on(k - 1)
    pass_on(shards - 1)
    for copy in to_sibling:
        copy.wait_recv()
    for copy in first:
        copy.wait_send()
    for copy in pending:
        copy.wait_send()
    own.wait()
    keep.wait()


def update_kernel(
    groups,
    owner, position, gathered, block, stat_left, stat_right,
    new_left, new_right, out,
    block_v, left_v, right_v, load_sem, store_sem, piece_sem,
):
    loads = [
        pltpu.make_async_copy(src, dst, load_sem.at[i])
        for i, (src, dst) in enumerate(
            [(block, block_v), (stat_left, left_v), (stat_right, right_v)])
    ]
    for copy in loads:
        copy.start()
    mine = lax.axis_index("shard") * groups + lax.axis_index("replica")
    count = owner.shape[0]
    moves = [
        pltpu.make_async_copy(gathered.at[owner[b]], out.at[position[b]], piece_sem.at[b])
        for b in range(count)
    ]
    for copy in moves:
        copy.start()
    hits = jnp.int32(0)
    for b in range(count):
        hits = hits + jnp.where(owner[b] == mine, 1, 0)
    occupied = hits > 0
    loads[0].wait()
    loads[1].wait()
    g = block_v[...]
    gram = lax.dot_general(g, g, (((1,), (1,)), ((), ())), preferred_element_type=jnp.float32)
    old = left_v[...]
    left_v[...] = jnp.where(occupied, BETA * old + (1.0 - BETA) * gram, old)
    store_left = pltpu.make_async_copy(left_v, new_left, store_sem.at[0])
    store_left.start()
    loads[2].wait()
    gram = lax.dot_general(g, g, (((0,), (0,)), ((), ())), preferred_element_type=jnp.float32)
    old = right_v[...]
    right_v[...] = jnp.where(occupied, BETA * old + (1.0 - BETA) * gram, old)
    store_right = pltpu.make_async_copy(right_v, new_right, store_sem.at[1])
    store_right.start()
    for copy in moves:
        copy.wait()
    store_left.wait()
    store_right.wait()


def body(shards, groups, grads, piece_position, owner, stat_left, stat_right, root_left, root_right):
    count = piece_position.shape[0]
    width = grads.shape[1]
    rows = grads.shape[0] // count
    chips = groups // CORES
    smem = pl.BlockSpec(memory_space=pltpu.SMEM)
    hbm = pl.BlockSpec(memory_space=pl.ANY)
    dma = pltpu.SemaphoreType.DMA
    square = (width, width)
    pieces = grads.reshape(count, rows, width)
    block, gathered = pl.pallas_call(
        functools.partial(exchange_kernel, shards, groups),
        out_shape=(
            jax.ShapeDtypeStruct((shards, rows, width), jnp.bfloat16),
            jax.ShapeDtypeStruct((shards * groups, rows, width), jnp.bfloat16),
        ),
        in_specs=[smem, smem, hbm, hbm, hbm],
        out_specs=(hbm, hbm),
        scratch_shapes=[
            pltpu.VMEM((count, rows, width), jnp.bfloat16),
            pltpu.VMEM(square, jnp.bfloat16),
            pltpu.VMEM(square, jnp.bfloat16),
            pltpu.VMEM((shards, rows, width), jnp.bfloat16),
            pltpu.VMEM((shards, rows, width), jnp.bfloat16),
            pltpu.VMEM((shards, rows, width), jnp.bfloat16),
            dma((3,)), dma, dma,
            dma((shards,)), dma((shards,)),
            dma((shards,)), dma((shards,)),
            dma((shards,)), dma((shards,)),
            dma((shards, chips)), dma((shards, chips)),
            dma((shards, chips)), dma((shards, chips)),
        ],
        compiler_params=pltpu.CompilerParams(
            collective_id=0, has_side_effects=True, vmem_limit_bytes=40 * 1024 * 1024),
        cost_estimate=pl.CostEstimate(
            flops=4 * width**3, bytes_accessed=8 * width * width * 2, transcendentals=0),
        name="exchange",
    )(owner, piece_position, pieces, root_left.reshape(square), root_right.reshape(square))

    new_left, new_right, out = pl.pallas_call(
        functools.partial(update_kernel, groups),
        out_shape=(
            jax.ShapeDtypeStruct(square, jnp.float32),
            jax.ShapeDtypeStruct(square, jnp.float32),
            jax.ShapeDtypeStruct((count, rows, width), jnp.bfloat16),
        ),
        in_specs=[smem, smem, hbm, hbm, hbm, hbm],
        out_specs=(hbm, hbm, hbm),
        scratch_shapes=[
            pltpu.VMEM(square, jnp.bfloat16),
            pltpu.VMEM(square, jnp.float32),
            pltpu.VMEM(square, jnp.float32),
            dma((3,)), dma((2,)), dma((count,)),
        ],
        compiler_params=pltpu.CompilerParams(vmem_limit_bytes=40 * 1024 * 1024),
        cost_estimate=pl.CostEstimate(
            flops=4 * width**3, bytes_accessed=20 * width * width, transcendentals=0),
        name="update",
    )(owner, piece_position, gathered, block.reshape(square),
      stat_left.reshape(square), stat_right.reshape(square))
    return (
        new_left.reshape(stat_left.shape),
        new_right.reshape(stat_right.shape),
        out.reshape(count * rows, width),
    )


def solution(mesh):
    slots = P("shard", "replica", None, None, None)
    return jax.shard_map(
        functools.partial(body, mesh.shape["shard"], mesh.shape["replica"]),
        mesh=mesh,
        in_specs=(P("shard", None), P(), P(), slots, slots, slots, slots),
        out_specs=(slots, slots, P("shard", None)),
        check_vma=False,
    )
```

time: 93.3 us -> 54.2 us (0.58)
  the two profiles are of different devices: /device:TPU:0 before, /device:TPU:19 now
where the time goes in v1:
time: 54.2 us; the launch traced here: 53.9 us
  Pallas kernels  48.2 us (89%)
  local copies, waits for them, and re-layouts  4.98 us (9%)
  between operations  0.67 us (1%)
    pallas_call x1, Pallas kernels, body(): pl.pallas_call(functools.partial(exchange_kernel, shards, groups), out_sh...  45.1 us
    unnamed x14, local copies, waits for them, and re-layouts  4.98 us
    pallas_call x1, Pallas kernels, body(): pl.pallas_call(functools.partial(update_kernel, groups), out_shape=(jax.S...  3.16 us

profile of v1, /device:TPU:19, one launch (start us, length us, event | category | flops | bytes accessed | tf_op | source)
XLA Modules:
  0.0 53.9 jit_solution(13418121043840218316)
XLA Ops:
  0.6 0.0 copy-start
  0.6 1.6 %copy-done = bf16[2048,512]{1,0:T(8,128)(2,1)S(1)} copy-done((bf16[2048,512]{1,0:T(8,128)(2,1)S(1)}, bf16[2048,512]{1,0:T(8,128)(2,1)}, u32[]{:S(2)}) %copy-start) | copy-done | bytes 2097176
  2.2 0.0 copy-start.3
  2.2 1.0 %copy-done.3 = bf16[1,1,1,512,512]{4,3,2,1,0:T(8,128)(2,1)S(1)} copy-done((bf16[1,1,1,512,512]{4,3,2,1,0:T(8,128)(2,1)S(1)}, bf16[1,1,1,512,512]{4,3,2,1,0:T(8,128)(2,1)}, u32[]{:S(2)}) %copy-start.3) | copy-done | bytes 524312
  3.3 0.0 copy-start.4
  3.3 1.0 %copy-done.4 = bf16[1,1,1,512,512]{4,3,2,1,0:T(8,128)(2,1)S(1)} copy-done((bf16[1,1,1,512,512]{4,3,2,1,0:T(8,128)(2,1)S(1)}, bf16[1,1,1,512,512]{4,3,2,1,0:T(8,128)(2,1)}, u32[]{:S(2)}) %copy-start.4) | copy-done | bytes 524312
  4.3 0.0 copy-start.5
  4.3 0.7 %copy-done.5 = s32[32]{0:T(128)S(1)} copy-done((s32[32]{0:T(128)S(1)}, s32[32]{0:T(128)}, u32[]{:S(2)}) %copy-start.5) | copy-done | bytes 152
  5.0 0.0 copy-start.6
  5.0 0.7 %copy-done.6 = s32[32]{0:T(128)S(1)} copy-done((s32[32]{0:T(128)S(1)}, s32[32]{0:T(128)}, u32[]{:S(2)}) %copy-start.6) | copy-done | bytes 152
  5.6 0.0 copy-start.1
  5.6 0.0 copy-start.2
  5.6 45.1 %exchange.1 = (bf16[8,64,512]{2,1,0:T(8,128)(2,1)S(1)}, bf16[32,64,512]{2,1,0:T(8,128)(2,1)S(1)}) custom-call(s32[32]{0:T(128)S(1)} %copy-done.5, s32[32]{0:T(128)S(1)} %copy-done.6, bf16[32,64,512]{2,1,0:T(8,128)(2,1)S(1)} %bitcast.9, bf16[512,512]{1,0:T(8,128)(2,1)S(1)} %bitcast.13, bf16[512,512]{1,0:T(8,128)(2,1)S(1)} %bitcast.14), custom_call_target="tpu_custom_call" | custom-call | flops 536870912 | bytes 4194304 | tf_op jit(solution)/shard_map/exchange/pallas_call | solution.py:205
  50.7 0.0 copy-done.1
  50.7 0.0 copy-done.2
  50.7 3.2 %update.1 = (f32[512,512]{1,0:T(8,128)}, f32[512,512]{1,0:T(8,128)}, bf16[32,64,512]{2,1,0:T(8,128)(2,1)}) custom-call(s32[32]{0:T(128)S(1)} %copy-done.5, s32[32]{0:T(128)S(1)} %copy-done.6, bf16[32,64,512]{2,1,0:T(8,128)(2,1)S(1)} %get-tuple-element.8.gathered, bf16[512,512]{1,0:T(8,128)(2,1)S(1)} %bitcast.12, f32[512,512]{1,0:T(8,128)S(1)} %bitcast.10, ...), custom_call_target="tpu_custom_call" | custom-call | flops 536870912 | bytes 5242880 | tf_op jit(solution)/shard_map/update/pallas_call | solution.py:234
Async XLA Ops:
  0.6 1.6 %copy-start = (bf16[2048,512]{1,0:T(8,128)(2,1)S(1)}, bf16[2048,512]{1,0:T(8,128)(2,1)}, u32[]{:S(2)}) copy-start(bf16[2048,512]{1,0:T(8,128)(2,1)} %param.7) | copy-start | bytes 6291460
  2.2 1.0 %copy-start.3 = (bf16[1,1,1,512,512]{4,3,2,1,0:T(8,128)(2,1)S(1)}, bf16[1,1,1,512,512]{4,3,2,1,0:T(8,128)(2,1)}, u32[]{:S(2)}) copy-start(bf16[1,1,1,512,512]{4,3,2,1,0:T(8,128)(2,1)} %param.12) | copy-start | bytes 1572868
  3.3 1.0 %copy-start.4 = (bf16[1,1,1,512,512]{4,3,2,1,0:T(8,128)(2,1)S(1)}, bf16[1,1,1,512,512]{4,3,2,1,0:T(8,128)(2,1)}, u32[]{:S(2)}) copy-start(bf16[1,1,1,512,512]{4,3,2,1,0:T(8,128)(2,1)} %param.13) | copy-start | bytes 1572868
  4.3 0.7 %copy-start.5 = (s32[32]{0:T(128)S(1)}, s32[32]{0:T(128)}, u32[]{:S(2)}) copy-start(s32[32]{0:T(128)} %owner.3) | copy-start | bytes 388
  5.0 0.7 %copy-start.6 = (s32[32]{0:T(128)S(1)}, s32[32]{0:T(128)}, u32[]{:S(2)}) copy-start(s32[32]{0:T(128)} %position.3) | copy-start | bytes 388
  5.6 45.1 %copy-start.1 = (f32[1,1,1,512,512]{4,3,2,1,0:T(8,128)S(1)}, f32[1,1,1,512,512]{4,3,2,1,0:T(8,128)}, u32[]{:S(2)}) copy-start(f32[1,1,1,512,512]{4,3,2,1,0:T(8,128)} %param.10) | copy-start | bytes 3145732
  5.6 45.1 %copy-start.2 = (f32[1,1,1,512,512]{4,3,2,1,0:T(8,128)S(1)}, f32[1,1,1,512,512]{4,3,2,1,0:T(8,128)}, u32[]{:S(2)}) copy-start(f32[1,1,1,512,512]{4,3,2,1,0:T(8,128)} %param.11) | copy-start | bytes 3145732

commit v2 on v1

v2 whole, which is shorter than its diff:
```python
import functools

import jax
import jax.numpy as jnp
from jax import lax
from jax.experimental import pallas as pl
from jax.experimental.pallas import tpu as pltpu
from jax.sharding import PartitionSpec as P

BETA = 0.95
MESH = pl.DeviceIdType.MESH
CORES = 2
VMEM_LIMIT = 40 * 1024 * 1024


def partner(me, k, shards):
    if shards & (shards - 1):
        return (shards + k - me) % shards
    bit, other = 1, me
    while bit < shards:
        if k & bit:
            other = other + bit * (1 - 2 * ((me // bit) % 2))
        bit *= 2
    return other


def exchange_kernel(
    shards, groups, order,
    owner, position, grads, root_left, root_right, stat_left, stat_right,
    new_left, new_right, gathered,
    owner_s, position_s, grads_v, left_v, right_v, outgoing, block, direction,
    load_sem, own_sem,
    send1, recv1, send2, recv2, send_sib, recv_sib, send_x, recv_x, send_xs, recv_xs,
):
    me = lax.axis_index("shard")
    group = lax.axis_index("replica")
    chips = groups // CORES
    sibling = group + 1 - 2 * (group % CORES)
    width = grads.shape[2]

    loads = [
        pltpu.make_async_copy(src, dst, load_sem.at[i])
        for i, (src, dst) in enumerate([
            (owner, owner_s), (position, position_s), (grads, grads_v),
            (root_left, left_v), (root_right, right_v),
            (stat_left, new_left), (stat_right, new_right)])
    ]
    for copy in loads[:3]:
        copy.start()

    barrier = pltpu.get_barrier_semaphore()
    for k in order:
        pl.semaphore_signal(
            barrier, inc=1, device_id={"shard": partner(me, k, shards), "replica": group},
            device_id_type=MESH)
    pl.semaphore_signal(
        barrier, inc=1, device_id={"shard": me, "replica": sibling}, device_id_type=MESH)
    for j in range(1, chips):
        pl.semaphore_signal(
            barrier, inc=1,
            device_id={"shard": me, "replica": (group + CORES * j) % groups},
            device_id_type=MESH)
    for copy in loads[3:]:
        copy.start()

    loads[0].wait()
    loads[1].wait()
    mine = me * groups + group
    targets = [((me + k) % shards) * groups + group for k in range(1, shards)]

    def find(b, carry):
        hits, own, found = carry
        o, p = owner_s[b], position_s[b]
        return (
            jnp.where(o == mine, 1, hits),
            jnp.where(o == mine, p, own),
            tuple(jnp.where(o == t, p, f) for t, f in zip(targets, found)),
        )

    zero = jnp.int32(0)
    hits, own, found = lax.fori_loop(
        0, owner.shape[0], find, (zero, zero, (zero,) * (shards - 1)), unroll=4)

    loads[2].wait()
    for k, f in enumerate(found, 1):
        outgoing[k] = grads_v[f]
    block[me] = grads_v[own]

    pl.semaphore_wait(barrier, shards + chips - 1)

    first = []
    for k in range(1, shards):
        copy = pltpu.make_async_remote_copy(
            src_ref=outgoing.at[k], dst_ref=block.at[me],
            send_sem=send1.at[k], recv_sem=recv1.at[k],
            device_id={"shard": (me + k) % shards, "replica": group}, device_id_type=MESH)
        copy.start()
        first.append(copy)
    for copy in loads[3:]:
        copy.wait()
    for copy in first:
        copy.wait_recv()

    whole = block[...].reshape(-1, width)
    half = jnp.dot(left_v[...], whole, preferred_element_type=jnp.float32).astype(jnp.bfloat16)
    direction[...] = jnp.dot(
        half, right_v[...], preferred_element_type=jnp.float32
    ).astype(jnp.bfloat16).reshape(direction.shape)

    pending = []
    second = {}
    across = {}
    to_sibling = []

    def send(source, slot, sends, recvs, shard, replica):
        copy = pltpu.make_async_remote_copy(
            src_ref=source, dst_ref=gathered.at[slot], send_sem=sends, recv_sem=recvs,
            device_id={"shard": shard, "replica": replica}, device_id_type=MESH)
        copy.start()
        pending.append(copy)
        return copy

    def send_across(k, source, slot):
        for j in range(1, chips):
            across[k, j] = send(
                source, slot, send_x.at[k, j], recv_x.at[k, j],
                me, (group + CORES * j) % groups)

    def send_second(k):
        other = partner(me, k, shards)
        second[k] = send(
            direction.at[other], mine, send2.at[k], recv2.at[k], other, group)

    def send_sibling(k, source, slot):
        to_sibling.append(send(source, slot, send_sib.at[k], recv_sib.at[k], me, sibling))

    def arrive(k):
        second[k].wait_recv()
        slot = partner(me, k, shards) * groups + group
        send_across(k, gathered.at[slot], slot)
        send_sibling(k, gathered.at[slot], slot)

    def pass_on(k):
        source_shard = partner(me, k, shards)
        for j in range(1, chips):
            across[k, j].wait_recv()
            slot = source_shard * groups + (group + groups - CORES * j) % groups
            to_sibling.append(send(
                gathered.at[slot], slot, send_xs.at[k, j], recv_xs.at[k, j], me, sibling))

    send_across(0, direction.at[me], mine)
    for k in order:
        send_second(k)
    send_sibling(0, direction.at[me], mine)
    own = pltpu.make_async_copy(direction.at[me], gathered.at[mine], own_sem)
    own.start()

    chunk = width // 4
    occupied = hits > 0
    for i in range(4):
        rows = pl.ds(i * chunk, chunk)
        gram = lax.dot_general(
            whole[i * chunk:(i + 1) * chunk], whole, (((1,), (1,)), ((), ())),
            preferred_element_type=jnp.float32)
        old = new_left[rows]
        new_left[rows] = jnp.where(occupied, BETA * old + (1.0 - BETA) * gram, old)
        gram = lax.dot_general(
            whole[:, i * chunk:(i + 1) * chunk], whole, (((0,), (0,)), ((), ())),
            preferred_element_type=jnp.float32)
        old = new_right[rows]
        new_right[rows] = jnp.where(occupied, BETA * old + (1.0 - BETA) * gram, old)

    last = 0
    for k in order:
        arrive(k)
        pass_on(last)
        last = k
    pass_on(last)
    for copy in to_sibling:
        copy.wait_recv()
    for copy in first:
        copy.wait_send()
    for copy in pending:
        copy.wait_send()
    own.wait()


def place_kernel(
    owner, position, gathered, left, right,
    new_left, new_right, out,
    store_sem, piece_sem,
):
    stores = [
        pltpu.make_async_copy(left, new_left, store_sem.at[0]),
        pltpu.make_async_copy(right, new_right, store_sem.at[1]),
    ]
    for copy in stores:
        copy.start()
    moves = [
        pltpu.make_async_copy(gathered.at[owner[b]], out.at[position[b]], piece_sem.at[b])
        for b in range(owner.shape[0])
    ]
    for copy in moves:
        copy.start()
    for copy in moves + stores:
        copy.wait()


def body(shards, groups, grads, piece_position, owner, stat_left, stat_right, root_left, root_right):
    count = piece_position.shape[0]
    width = grads.shape[1]
    rows = grads.shape[0] // count
    chips = groups // CORES
    order = tuple(range(1, shards))
    smem = pl.BlockSpec(memory_space=pltpu.SMEM)
    hbm = pl.BlockSpec(memory_space=pltpu.HBM)
    anywhere = pl.BlockSpec(memory_space=pl.ANY)
    vmem = pl.BlockSpec(memory_space=pltpu.VMEM)
    dma = pltpu.SemaphoreType.DMA
    square = (width, width)
    pieces = grads.reshape(count, rows, width)
    left, right, gathered = pl.pallas_call(
        functools.partial(exchange_kernel, shards, groups, order),
        out_shape=(
            jax.ShapeDtypeStruct(square, jnp.float32),
            jax.ShapeDtypeStruct(square, jnp.float32),
            jax.ShapeDtypeStruct((shards * groups, rows, width), jnp.bfloat16),
        ),
        in_specs=[hbm] * 7,
        out_specs=(vmem, vmem, anywhere),
        scratch_shapes=[
            pltpu.SMEM((count,), jnp.int32),
            pltpu.SMEM((count,), jnp.int32),
            pltpu.VMEM((count, rows, width), jnp.bfloat16),
            pltpu.VMEM(square, jnp.bfloat16),
            pltpu.VMEM(square, jnp.bfloat16),
            pltpu.VMEM((shards, rows, width), jnp.bfloat16),
            pltpu.VMEM((shards, rows, width), jnp.bfloat16),
            pltpu.VMEM((shards, rows, width), jnp.bfloat16),
            dma((7,)), dma,
            dma((shards,)), dma((shards,)),
            dma((shards,)), dma((shards,)),
            dma((shards,)), dma((shards,)),
            dma((shards, chips)), dma((shards, chips)),
            dma((shards, chips)), dma((shards, chips)),
        ],
        compiler_params=pltpu.CompilerParams(
            collective_id=0, has_side_effects=True, vmem_limit_bytes=VMEM_LIMIT),
        cost_estimate=pl.CostEstimate(
            flops=8 * width**3, bytes_accessed=24 * width * width, transcendentals=0),
        name="exchange",
    )(*[pltpu.with_memory_space_constraint(x, pltpu.HBM) for x in (
        owner, piece_position, pieces, root_left.reshape(square), root_right.reshape(square),
        stat_left.reshape(square), stat_right.reshape(square))])

    new_left, new_right, out = pl.pallas_call(
        place_kernel,
        out_shape=(
            jax.ShapeDtypeStruct(square, jnp.float32),
            jax.ShapeDtypeStruct(square, jnp.float32),
            jax.ShapeDtypeStruct((count, rows, width), jnp.bfloat16),
        ),
        in_specs=[smem, smem, anywhere, anywhere, anywhere],
        out_specs=(hbm, hbm, hbm),
        scratch_shapes=[dma((2,)), dma((count,))],
        compiler_params=pltpu.CompilerParams(vmem_limit_bytes=16 * 1024 * 1024),
        cost_estimate=pl.CostEstimate(
            flops=0, bytes_accessed=16 * width * width, transcendentals=0),
        name="place",
    )(owner, piece_position, gathered, left, right)
    return (
        new_left.reshape(stat_left.shape),
        new_right.reshape(stat_right.shape),
        out.reshape(count * rows, width),
    )


def solution(mesh):
    slots = P("shard", "replica", None, None, None)
    return jax.shard_map(
        functools.partial(body, mesh.shape["shard"], mesh.shape["replica"]),
        mesh=mesh,
        in_specs=(P("shard", None), P(), P(), slots, slots, slots, slots),
        out_specs=(slots, slots, P("shard", None)),
        check_vma=False,
    )
```

time: 54.2 us -> 43.6 us (0.80)
  the two profiles are of different devices: /device:TPU:19 before, /device:TPU:0 now
where the time goes in v2:
time: 43.6 us; the launch traced here: 43.4 us
  Pallas kernels  42.8 us (98%)
  between operations  0.67 us (2%)
    pallas_call x1, Pallas kernels, body(): pl.pallas_call(functools.partial(exchange_kernel, shards, groups, order),...  39.9 us
    pallas_call x1, Pallas kernels, body(): pl.pallas_call(place_kernel, out_shape=(jax.ShapeDtypeStruct(square, jnp....  2.83 us

profile of v2, /device:TPU:0, one launch (start us, length us, event | category | flops | bytes accessed | tf_op | source)
XLA Modules:
  0.0 43.4 jit_solution(7067890935821453000)
XLA Ops:
  0.6 0.0 copy-start
  0.6 0.0 copy-start.1
  0.7 39.9 %exchange.1 = (f32[512,512]{1,0:T(8,128)S(1)}, f32[512,512]{1,0:T(8,128)S(1)}, bf16[32,64,512]{2,1,0:T(8,128)(2,1)S(1)}) custom-call(s32[32]{0:T(128)} %owner.3, s32[32]{0:T(128)} %position.3, bf16[32,64,512]{2,1,0:T(8,128)(2,1)} %bitcast.8, bf16[512,512]{1,0:T(8,128)(2,1)} %bitcast.11, bf16[512,512]{1,0:T(8,128)(2,1)} %bitcast.12, f32[512,512]{1,0:T(8,128)} %bitcast.9, ...), custom_call_target="tpu_custom_call" | custom-call | flops 1073741824 | bytes 6291456 | tf_op jit(solution)/shard_map/exchange/pallas_call | solution.py:222
  40.6 0.0 copy-done
  40.6 0.0 copy-done.1
  40.6 2.8 %place.1 = (f32[512,512]{1,0:T(8,128)}, f32[512,512]{1,0:T(8,128)}, bf16[32,64,512]{2,1,0:T(8,128)(2,1)}) custom-call(s32[32]{0:T(128)S(1)} %copy-done, s32[32]{0:T(128)S(1)} %copy-done.1, bf16[32,64,512]{2,1,0:T(8,128)(2,1)S(1)} %get-tuple-element.9.gathered, f32[512,512]{1,0:T(8,128)S(1)} %get-tuple-element.10.left, f32[512,512]{1,0:T(8,128)S(1)} %get-tuple-element.11.right), custom_call_target="tpu_custom_call" | custom-call | bytes 4194304 | tf_op jit(solution)/shard_map/place/pallas_call | solution.py:256
Async XLA Ops:
  0.6 40.0 %copy-start = (s32[32]{0:T(128)S(1)}, s32[32]{0:T(128)}, u32[]{:S(2)}) copy-start(s32[32]{0:T(128)} %owner.3) | copy-start | bytes 388
  0.6 40.0 %copy-start.1 = (s32[32]{0:T(128)S(1)}, s32[32]{0:T(128)}, u32[]{:S(2)}) copy-start(s32[32]{0:T(128)} %position.3) | copy-start | bytes 388

commit v3 on v2

--- a/solution.py
+++ b/solution.py
@@ -149,7 +149,7 @@
                 gathered.at[slot], slot, send_xs.at[k, j], recv_xs.at[k, j], me, sibling))
 
     send_across(0, direction.at[me], mine)
-    for k in order:
+    for k in order[:3]:
         send_second(k)
     send_sibling(0, direction.at[me], mine)
     own = pltpu.make_async_copy(direction.at[me], gathered.at[mine], own_sem)
@@ -170,12 +170,16 @@
         old = new_right[rows]
         new_right[rows] = jnp.where(occupied, BETA * old + (1.0 - BETA) * gram, old)
 
-    last = 0
-    for k in order:
+    waiting = [0]
+    for n, k in enumerate(order):
+        if n + 3 < len(order):
+            send_second(order[n + 3])
         arrive(k)
-        pass_on(last)
-        last = k
-    pass_on(last)
+        waiting.append(k)
+        if len(waiting) > 3:
+            pass_on(waiting.pop(0))
+    for k in waiting:
+        pass_on(k)
     for copy in to_sibling:
         copy.wait_recv()
     for copy in first:

time: 43.6 us -> 40 us (0.917)
  Pallas kernels: 42.8 us -> 38.8 us
    pallas_call x1, Pallas kernels: 39.9 us -> 36 us  [body(): pl.pallas_call(functools.partial(exchange_kernel, shards, groups, order),...]
where the time goes in v3:
time: 40 us; the launch traced here: 39.5 us
  Pallas kernels  38.8 us (97%)
  between operations  0.67 us (2%)
    pallas_call x1, Pallas kernels, body(): pl.pallas_call(functools.partial(exchange_kernel, shards, groups, order),...  36 us
    pallas_call x1, Pallas kernels, body(): pl.pallas_call(place_kernel, out_shape=(jax.ShapeDtypeStruct(square, jnp....  2.83 us

profile of v3, /device:TPU:0, one launch (start us, length us, event | category | flops | bytes accessed | tf_op | source)
XLA Modules:
  0.0 39.5 jit_solution(8135782828504869268)
XLA Ops:
  0.6 0.0 copy-start
  0.6 0.0 copy-start.1
  0.7 36.0 %exchange.1 = (f32[512,512]{1,0:T(8,128)S(1)}, f32[512,512]{1,0:T(8,128)S(1)}, bf16[32,64,512]{2,1,0:T(8,128)(2,1)S(1)}) custom-call(s32[32]{0:T(128)} %owner.3, s32[32]{0:T(128)} %position.3, bf16[32,64,512]{2,1,0:T(8,128)(2,1)} %bitcast.8, bf16[512,512]{1,0:T(8,128)(2,1)} %bitcast.11, bf16[512,512]{1,0:T(8,128)(2,1)} %bitcast.12, f32[512,512]{1,0:T(8,128)} %bitcast.9, ...), custom_call_target="tpu_custom_call" | custom-call | flops 1073741824 | bytes 6291456 | tf_op jit(solution)/shard_map/exchange/pallas_call | solution.py:226
  36.7 0.0 copy-done
  36.7 0.0 copy-done.1
  36.7 2.8 %place.1 = (f32[512,512]{1,0:T(8,128)}, f32[512,512]{1,0:T(8,128)}, bf16[32,64,512]{2,1,0:T(8,128)(2,1)}) custom-call(s32[32]{0:T(128)S(1)} %copy-done, s32[32]{0:T(128)S(1)} %copy-done.1, bf16[32,64,512]{2,1,0:T(8,128)(2,1)S(1)} %get-tuple-element.9.gathered, f32[512,512]{1,0:T(8,128)S(1)} %get-tuple-element.10.left, f32[512,512]{1,0:T(8,128)S(1)} %get-tuple-element.11.right), custom_call_target="tpu_custom_call" | custom-call | bytes 4194304 | tf_op jit(solution)/shard_map/place/pallas_call | solution.py:260
Async XLA Ops:
  0.6 36.0 %copy-start = (s32[32]{0:T(128)S(1)}, s32[32]{0:T(128)}, u32[]{:S(2)}) copy-start(s32[32]{0:T(128)} %owner.3) | copy-start | bytes 388
  0.6 36.0 %copy-start.1 = (s32[32]{0:T(128)S(1)}, s32[32]{0:T(128)}, u32[]{:S(2)}) copy-start(s32[32]{0:T(128)} %position.3) | copy-start | bytes 388

commit v4 on v3

--- a/solution.py
+++ b/solution.py
@@ -29,7 +29,7 @@
     owner, position, grads, root_left, root_right, stat_left, stat_right,
     new_left, new_right, gathered,
     owner_s, position_s, grads_v, left_v, right_v, outgoing, block, direction,
-    load_sem, own_sem,
+    load_sem, fetch_sem, own_sem,
     send1, recv1, send2, recv2, send_sib, recv_sib, send_x, recv_x, send_xs, recv_xs,
 ):
     me = lax.axis_index("shard")
@@ -41,11 +41,18 @@
     loads = [
         pltpu.make_async_copy(src, dst, load_sem.at[i])
         for i, (src, dst) in enumerate([
-            (owner, owner_s), (position, position_s), (grads, grads_v),
+            (owner, owner_s), (position, position_s),
             (root_left, left_v), (root_right, right_v),
             (stat_left, new_left), (stat_right, new_right)])
     ]
-    for copy in loads[:3]:
+    quarter = grads.shape[0] // 4
+    fetches = [
+        pltpu.make_async_copy(
+            grads.at[pl.ds(i * quarter, quarter)], grads_v.at[pl.ds(i * quarter, quarter)],
+            fetch_sem.at[i])
+        for i in range(4)
+    ]
+    for copy in loads[:2] + fetches:
         copy.start()
 
     barrier = pltpu.get_barrier_semaphore()
@@ -60,8 +67,6 @@
             barrier, inc=1,
             device_id={"shard": me, "replica": (group + CORES * j) % groups},
             device_id_type=MESH)
-    for copy in loads[3:]:
-        copy.start()
 
     loads[0].wait()
     loads[1].wait()
@@ -81,7 +86,8 @@
     hits, own, found = lax.fori_loop(
         0, owner.shape[0], find, (zero, zero, (zero,) * (shards - 1)), unroll=4)
 
-    loads[2].wait()
+    for copy in fetches:
+        copy.wait()
     for k, f in enumerate(found, 1):
         outgoing[k] = grads_v[f]
     block[me] = grads_v[own]
@@ -96,7 +102,9 @@
             device_id={"shard": (me + k) % shards, "replica": group}, device_id_type=MESH)
         copy.start()
         first.append(copy)
-    for copy in loads[3:]:
+    for copy in loads[2:]:
+        copy.start()
+    for copy in loads[2:]:
         copy.wait()
     for copy in first:
         copy.wait_recv()
@@ -241,7 +249,7 @@
             pltpu.VMEM((shards, rows, width), jnp.bfloat16),
             pltpu.VMEM((shards, rows, width), jnp.bfloat16),
             pltpu.VMEM((shards, rows, width), jnp.bfloat16),
-            dma((7,)), dma,
+            dma((6,)), dma((4,)), dma,
             dma((shards,)), dma((shards,)),
             dma((shards,)), dma((shards,)),
             dma((shards,)), dma((shards,)),

time: 40 us -> 40.2 us (level)
  no operation moved by 1% of the time
where the time goes in v4:
time: 40.2 us; the launch traced here: 39.5 us
  Pallas kernels  38.9 us (97%)
  between operations  0.67 us (2%)
    pallas_call x1, Pallas kernels, body(): pl.pallas_call(functools.partial(exchange_kernel, shards, groups, order),...  36 us
    pallas_call x1, Pallas kernels, body(): pl.pallas_call(place_kernel, out_shape=(jax.ShapeDtypeStruct(square, jnp....  2.83 us

profile of v4, /device:TPU:0, one launch (start us, length us, event | category | flops | bytes accessed | tf_op | source)
XLA Modules:
  0.0 39.5 jit_solution(6051395392357922589)
XLA Ops:
  0.6 0.0 copy-start
  0.6 0.0 copy-start.1
  0.7 36.0 %exchange.1 = (f32[512,512]{1,0:T(8,128)S(1)}, f32[512,512]{1,0:T(8,128)S(1)}, bf16[32,64,512]{2,1,0:T(8,128)(2,1)S(1)}) custom-call(s32[32]{0:T(128)} %owner.3, s32[32]{0:T(128)} %position.3, bf16[32,64,512]{2,1,0:T(8,128)(2,1)} %bitcast.8, bf16[512,512]{1,0:T(8,128)(2,1)} %bitcast.11, bf16[512,512]{1,0:T(8,128)(2,1)} %bitcast.12, f32[512,512]{1,0:T(8,128)} %bitcast.9, ...), custom_call_target="tpu_custom_call" | custom-call | flops 1073741824 | bytes 6291456 | tf_op jit(solution)/shard_map/exchange/pallas_call | solution.py:234
  36.7 0.0 copy-done
  36.7 0.0 copy-done.1
  36.7 2.8 %place.1 = (f32[512,512]{1,0:T(8,128)}, f32[512,512]{1,0:T(8,128)}, bf16[32,64,512]{2,1,0:T(8,128)(2,1)}) custom-call(s32[32]{0:T(128)S(1)} %copy-done, s32[32]{0:T(128)S(1)} %copy-done.1, bf16[32,64,512]{2,1,0:T(8,128)(2,1)S(1)} %get-tuple-element.9.gathered, f32[512,512]{1,0:T(8,128)S(1)} %get-tuple-element.10.left, f32[512,512]{1,0:T(8,128)S(1)} %get-tuple-element.11.right), custom_call_target="tpu_custom_call" | custom-call | bytes 4194304 | tf_op jit(solution)/shard_map/place/pallas_call | solution.py:268
Async XLA Ops:
  0.6 36.1 %copy-start = (s32[32]{0:T(128)S(1)}, s32[32]{0:T(128)}, u32[]{:S(2)}) copy-start(s32[32]{0:T(128)} %owner.3) | copy-start | bytes 388
  0.6 36.1 %copy-start.1 = (s32[32]{0:T(128)S(1)}, s32[32]{0:T(128)}, u32[]{:S(2)}) copy-start(s32[32]{0:T(128)} %position.3) | copy-start | bytes 388
